TPU v7x, 32 devices: a whole 2x2x4 slice. The times are simulated.
32 devices in a mesh: mp: 2 (over x), dp: 4 (over y, core), tensor: 4 (over z).
Axes of the slice: x: 2, y: 2, z: 4, core: 2. Of those that a mesh axis runs over, the one named last changes fastest.
Arguments:
- activations: bfloat16 [2, 512, 8192], P('mp', 'dp'), may hold values from -6 to 6
- gate_pre: bfloat16 [2, 512, 28672], P('mp', 'dp', 'tensor'), may hold values from -6 to 6
- hidden_grad: bfloat16 [2, 512, 28672], P('mp', 'dp', 'tensor'), may hold values from -1.2 to 1.2, as said below
- up_weights: bfloat16 [2, 8192, 28672], P('mp', 'dp', 'tensor'), may hold values from -6 to 6
Outputs:
- merged: bfloat16 [8192, 28672], P(('dp', 'mp'), 'tensor')
Inputs may be any that keep to these rules, and one draw needn't show every extreme that they name: `hidden_grad`: each sequence's values share one scale, spread evenly in the logarithm between 0.005 and 0.3 over sequences.
All inputs are finite; a program needn't handle non-finite values.
Results may differ from a plain program's by a relative error of at most 0.003.
Values may be sent and summed in bfloat16 or wider, within the bound.
A program may use at most 320 MiB of HBM per device.

v0:
```python
import math

import jax
import jax.numpy as jnp
from jax import lax
from jax.sharding import PartitionSpec as P

D = 8192
FF = 28672
LEN = 128


clip_ratio = 0.05
fisher_floor = 0.1


def for_sending(value):

    def short(part):
        return part.astype(jnp.bfloat16) if part.dtype == jnp.float32 else part

    return jax.tree.map(short, value)


def local(activations, gate_pre, hidden_grad, up_weights):
    single_precision = jnp.float32
    input_row_block = activations[0]
    tokens_per_worker, width = input_row_block.shape
    seq_dev = tokens_per_worker // LEN
    cot = (
        hidden_grad[0].astype(single_precision) * jax.nn.silu(gate_pre[0].astype(single_precision))
    ).astype(jnp.bfloat16)
    cot_seq = cot.reshape(seq_dev, LEN, cot.shape[1])
    sequence_inputs = input_row_block.reshape(seq_dev, LEN, width)
    input_gram_matrix = jnp.einsum(
        "tpe,txe->tpx", sequence_inputs, sequence_inputs, preferred_element_type=single_precision
    )
    gram_local = jnp.einsum(
        "slf,smf->slm", cot_seq, cot_seq, preferred_element_type=single_precision
    )
    gram_cot = lax.psum(gram_local, "tensor")
    grad_norm = jnp.sqrt(jnp.sum(input_gram_matrix * gram_cot, axis=(1, 2)))
    clip_limit = clip_ratio * math.sqrt(LEN * D * FF)
    factor = clip_limit / jnp.maximum(grad_norm, clip_limit)
    clip_sq = factor * factor
    row_block = lax.all_to_all(input_row_block, "dp", split_axis=1, concat_axis=0, tiled=True)
    both_acts = lax.all_to_all(row_block[None], "mp", split_axis=2, concat_axis=0, tiled=True)
    both_weights = lax.all_to_all(up_weights, "mp", split_axis=1, concat_axis=0, tiled=True)
    both_cot, both_clip = (
        lax.all_gather(cot_seq[None], "mp", axis=0, tiled=True),
        lax.all_gather(clip_sq[None].astype(jnp.bfloat16), "mp", axis=0, tiled=True).astype(
            jnp.float32
        ),
    )
    model_total_count = both_acts.shape[0]
    acts_models = both_acts.reshape(model_total_count, -1, LEN, both_acts.shape[2])
    start_both = jnp.zeros(both_weights.shape, single_precision)
    cot_piece = lax.all_gather(both_cot, "dp", axis=1, tiled=True)
    scale_piece = lax.all_gather(for_sending(both_clip), "dp", axis=1, tiled=True)
    count = cot_piece.shape[1]

    def one_seq(seq_index, total):
        grad = jnp.einsum(
            "mld,mlf->mdf",
            acts_models[:, seq_index],
            cot_piece[:, seq_index],
            preferred_element_type=single_precision,
        )
        return total + scale_piece[:, seq_index, None, None] * grad * grad

    fisher_both = lax.fori_loop(0, count, one_seq, start_both)
    weighted = fisher_both + fisher_floor
    numer = jnp.sum(weighted * both_weights.astype(single_precision), axis=0)
    denom = jnp.sum(weighted, axis=0)
    return (numer / denom).astype(jnp.bfloat16)


def solution(mesh):
    placed = (
        P("mp", "dp", None),
        P("mp", "dp", "tensor"),
        P("mp", "dp", "tensor"),
        P("mp", "dp", "tensor"),
    )
    return jax.shard_map(
        local, mesh=mesh, in_specs=placed, out_specs=P(("dp", "mp"), "tensor"), check_vma=False
    )
```

profile of v0, /device:TPU:0, one launch (start us, length us, event | category | flops | bytes accessed | tf_op | source)
XLA Modules:
  0.0 1110.2 jit_solution(10786797215222230430)
XLA Ops:
  7.4 4.5 fusion.17
  12.0 4.9 fusion.23
  17.0 48.7 %all-gather.4.cloned.1.call-done = bf16[2,1,128,7168]{3,2,1,0:T(8,128)(2,1)} async-done(((bf16[1,1,128,7168]{3,2,1,0:T(8,128)(2,1)}), bf16[2,1,128,7168]{3,2,1,0:T(8,128)(2,1)}) %all-gather.4.cloned.1.call-update) | async-done | bytes 3670032 | tf_op jit(solution)/shard_map/all_gather | solution.py:50
  65.7 3.2 copy.29
  68.9 46.4 %all_to_all.40 = bf16[128,4,2048]{0,2,1:T(8,128)(2,1)} all-to-all(bf16[128,4,2048]{0,2,1:T(8,128)(2,1)S(1)} %bitcast.93), channel_id=1, replica_groups=mesh['mp'=2,'dp'=4,'tensor'=4] {'dp'}, dimensions={1} | all-to-all | bytes 4194304 | tf_op jit(solution)/shard_map/all_to_all | solution.py:46
  115.3 2.9 copy.30
  118.2 7.5 copy.31
  126.3 14.1 %reduce.2 = bf16[2048,512]{1,0:T(8,128)(2,1)S(1)} reduce(bf16[2048,1,512]{2,1,0:T(2,128)(2,1)} %bitcast.87, bf16[]{:T(256)} %broadcast.25), dimensions={1}, to_apply=%bitcast.74.reduce_sub_computation | reduce | bytes 4194306
  140.4 2.5 reshape.112
  142.9 3.9 all-to-all-start.1
  146.9 50.4 %copy.42 = bf16[1,2048,7168]{2,0,1:T(2,128)(2,1)} copy(bf16[1,2048,7168]{2,1,0:T(8,128)(2,1)} %param.9) | data formatting | bytes 58720256 | tf_op args[3]
  197.3 173.3 %reduce.1 = bf16[2048,7168]{1,0:T(8,128)(2,1)} reduce(bf16[2048,1,7168]{2,1,0:T(2,128)(2,1)} %bitcast.84, bf16[]{:T(256)} %broadcast.25), dimensions={1}, to_apply=%bitcast.77.reduce_sub_computation | reduce | bytes 58720256
  370.6 46.4 %reshape.110 = bf16[2,2,3670016]{2,1,0:T(2,128)(2,1)} reshape(bf16[2048,7168]{1,0:T(8,128)(2,1)} %reduce.1) | data formatting | bytes 58720256
  417.0 12.6 %all-to-all-start.2 = ((bf16[2,2,3670016]{2,1,0:T(2,128)(2,1)}), bf16[2,2,3670016]{2,1,0:T(2,128)(2,1)}, u32[]{:S(2)}, u32[]{:S(2)}) async-start(bf16[2,2,3670016]{2,1,0:T(2,128)(2,1)} %reshape.110), calls=%async_computation.2 | async-start | bytes 58720256 | tf_op jit(solution)/shard_map/all_to_all | solution.py:48
  429.6 0.6 dynamic-slice
  430.2 3.5 fusion.32
  434.5 0.8 dynamic-update-slice
  435.2 310.9 %all-reduce = bf16[2]{0:T(256)(128)(2,1)S(1)} all-reduce(bf16[2]{0:T(256)(128)(2,1)S(1)} %dynamic-update-slice), channel_id=1, replica_groups=mesh['mp'=2,'dp'=4,'tensor'=4] {'mp'}, use_global_device_ids=true, to_apply=%add | all-reduce | flops 2 | bytes 8
  746.2 5.0 all-gather
  751.3 3.5 reshape.113
  754.8 4.1 copy.40
  758.9 3.0 copy.32
  761.9 67.2 %reshape.111 = bf16[2048,1,7168]{2,1,0:T(2,128)(2,1)} reshape(bf16[2,2,3670016]{2,1,0:T(2,128)(2,1)} %all-to-all-done.2) | data formatting | bytes 58720256
  829.2 30.4 %copy.37 = bf16[1,2048,7168]{2,1,0:T(8,128)(2,1)} copy(bf16[1,2048,7168]{2,0,1:T(2,128)(2,1)} %bitcast.85) | data formatting | bytes 58720256 | tf_op jit(solution)/shard_map/all_to_all | solution.py:48
  859.6 142.1 %while.14 = (s32[]{:T(128)}, f32[2,1024,7168]{2,1,0:T(8,128)}, bf16[2,4]{1,0:T(2,128)(2,1)S(1)}, bf16[2,4,128,1024]{3,2,1,0:T(8,128)(2,1)S(1)}, bf16[2,4,128,7168]{3,2,0,1:T(8,128)(2,1)}, /*index=5*/s32[]{:T(128)}, s32[]{:T(128)}) while((s32[]{:T(128)}, f32[2,1024,7168]{2,1,0:T(8,128)}, bf16[2,4]{1,0:T(2,128)(2,1)S(1)}, ...), condition=%wide.region_3.4_spmd.clone, body=%wide.region_2.3_spmd.clone.sunk | while | flops 3816816640 | bytes 121636472 | solution.py:71
  859.8 22.2 %fusion.41 = f32[2,1024,7168]{2,1,0:T(8,128)} fusion(f32[2,1024,7168]{2,1,0:T(8,128)} %get-tuple-element.192, f32[2]{0:T(128)S(1)} %bitcast_convert_fusion.2, pred[]{:T(512)S(6)} %compare.3, bf16[2,4,128,7168]{3,2,0,1:T(8,128)(2,1)} %get-tuple-element.202, s32[]{:T(128)} %get-tuple-element.191, bf16[2,4,128,1024]{3,2,1,0:T(8,128)(2,1)S(1)} %get-tuple-element.201), kind=kOutput, calls=%fused_computation.1.clone.1 | convolution fusion | flops 3816816640 | bytes 121636352 | tf_op jit(solution)/shard_map/while/body/eval_jaxpr/mld,mlf->mdf/dot_general | solution.py:63
  882.1 39.7 %fusion.41 = f32[2,1024,7168]{2,1,0:T(8,128)} fusion(f32[2,1024,7168]{2,1,0:T(8,128)} %get-tuple-element.192, f32[2]{0:T(128)S(1)} %bitcast_convert_fusion.2, pred[]{:T(512)S(6)} %compare.3, bf16[2,4,128,7168]{3,2,0,1:T(8,128)(2,1)} %get-tuple-element.202, s32[]{:T(128)} %get-tuple-element.191, bf16[2,4,128,1024]{3,2,1,0:T(8,128)(2,1)S(1)} %get-tuple-element.201), kind=kOutput, calls=%fused_computation.1.clone.1 | convolution fusion | flops 3816816640 | bytes 121636352 | tf_op jit(solution)/shard_map/while/body/eval_jaxpr/mld,mlf->mdf/dot_general | solution.py:63
  922.1 39.7 %fusion.41 = f32[2,1024,7168]{2,1,0:T(8,128)} fusion(f32[2,1024,7168]{2,1,0:T(8,128)} %get-tuple-element.192, f32[2]{0:T(128)S(1)} %bitcast_convert_fusion.2, pred[]{:T(512)S(6)} %compare.3, bf16[2,4,128,7168]{3,2,0,1:T(8,128)(2,1)} %get-tuple-element.202, s32[]{:T(128)} %get-tuple-element.191, bf16[2,4,128,1024]{3,2,1,0:T(8,128)(2,1)S(1)} %get-tuple-element.201), kind=kOutput, calls=%fused_computation.1.clone.1 | convolution fusion | flops 3816816640 | bytes 121636352 | tf_op jit(solution)/shard_map/while/body/eval_jaxpr/mld,mlf->mdf/dot_general | solution.py:63
  962.0 39.7 %fusion.41 = f32[2,1024,7168]{2,1,0:T(8,128)} fusion(f32[2,1024,7168]{2,1,0:T(8,128)} %get-tuple-element.192, f32[2]{0:T(128)S(1)} %bitcast_convert_fusion.2, pred[]{:T(512)S(6)} %compare.3, bf16[2,4,128,7168]{3,2,0,1:T(8,128)(2,1)} %get-tuple-element.202, s32[]{:T(128)} %get-tuple-element.191, bf16[2,4,128,1024]{3,2,1,0:T(8,128)(2,1)S(1)} %get-tuple-element.201), kind=kOutput, calls=%fused_computation.1.clone.1 | convolution fusion | flops 3816816640 | bytes 121636352 | tf_op jit(solution)/shard_map/while/body/eval_jaxpr/mld,mlf->mdf/dot_general | solution.py:63
  1001.7 35.2 %add_reduce_fusion = f32[1024,7168]{1,0:T(8,128)} fusion(f32[2,1024,7168]{2,1,0:T(8,128)} %get-tuple-element.99), kind=kLoop, calls=%fused_computation.11 | loop fusion | flops 22020096 | bytes 88080384 | tf_op jit(solution)/shard_map/reduce_sum | solution.py:74
  1037.0 41.0 %fusion.6 = f32[1024,7168]{1,0:T(8,128)} fusion(bf16[2,1024,7168]{2,1,0:T(8,128)(2,1)} %bitcast.86, f32[2,1024,7168]{2,1,0:T(8,128)} %get-tuple-element.99), kind=kLoop, calls=%fused_computation.10 | loop fusion | flops 51380224 | bytes 117440512 | tf_op jit(solution)/shard_map/reduce_sum | solution.py:73
  1077.9 24.7 %divide_convert_fusion = bf16[1024,7168]{1,0:T(8,128)(2,1)} fusion(f32[1024,7168]{1,0:T(8,128)} %fusion.6, f32[1024,7168]{1,0:T(8,128)} %add_reduce_fusion), kind=kLoop, calls=%fused_computation.12 | loop fusion | flops 14680064 | bytes 73400320 | tf_op jit(solution)/shard_map/convert_element_type | solution.py:75
  (30 shorter events, 1.6 us)
Async XLA Ops:
  7.4 4.6 copy-start
  7.4 58.3 %all-gather.4.cloned.1.call-start = ((), (), s32[]{:S(2)}) async-start(), calls=%async_computation.4 | async-start | bytes 5505024 | tf_op jit(solution)/shard_map/all_gather | solution.py:50
  11.9 418.3 %all-reduce.3.cloned.1.call-start = ((), (), s32[]{:S(2)}) async-start(), calls=%async_computation.3 | async-start | bytes 131072 | tf_op jit(solution)/shard_map/psum | solution.py:41
  16.9 842.7 %all-gather.6.cloned.1.call-start = ((), (), s32[]{:S(2)}) async-start(), calls=%async_computation.5 | async-start | bytes 18350080 | tf_op jit(solution)/shard_map/all_gather | solution.py:58
  142.9 274.0 %all-to-all-start.1 = ((bf16[2,2,262144]{2,1,0:T(2,128)(2,1)}), bf16[2,2,262144]{2,1,0:T(2,128)(2,1)S(1)}, u32[]{:S(2)}, u32[]{:S(2)}) async-start(bf16[2,2,262144]{2,1,0:T(2,128)(2,1)} %reshape.112), calls=%async_computation.1 | async-start | bytes 4194304 | tf_op jit(solution)/shard_map/all_to_all | solution.py:47
  417.0 12.6 %copy-start.1 = (u32[32]{0:T(128)S(1)}, u32[32]{0:T(128)}, u32[]{:S(2)}) copy-start(u32[32]{0:T(128)} %constant.42) | copy-start | bytes 388
  417.0 344.9 %all-to-all-start.2 = ((bf16[2,2,3670016]{2,1,0:T(2,128)(2,1)}), bf16[2,2,3670016]{2,1,0:T(2,128)(2,1)}, u32[]{:S(2)}, u32[]{:S(2)}) async-start(bf16[2,2,3670016]{2,1,0:T(2,128)(2,1)} %reshape.110), calls=%async_computation.2 | async-start | bytes 58720256 | tf_op jit(solution)/shard_map/all_to_all | solution.py:48
Sparse Core Ops, SparseCore 0:
  12.0 53.5 all-gather.3
  67.3 111.1 all-gather.5
Sparse Core Ops, SparseCore 1:
  17.0 36.5 all-reduce.2
where the time goes:
time: 1120 us; the launch traced here: 1110 us
  blocking collectives  362 us (32%)
  other arithmetic  293 us (26%)
  local copies, waits for them, and re-layouts  224 us (20%)
  matrix products  150 us (13%)
  waiting for transfers between devices  48.7 us (4%)
  starting transfers between devices  16.6 us (1%)
  between operations  15.9 us (1%)
    unnamed x1, blocking collectives  311 us
    unnamed x3, other arithmetic  187 us
    unnamed x15, local copies, waits for them, and re-layouts  179 us
    dot_general x4, matrix products, one_seq(): jnp.einsum('mld,mlf->mdf', acts_models[:, seq_index], cot_piece[:, seq_in...  141 us
    all_gather x1, waiting for transfers between devices, local(): lax.all_gather(cot_seq[None], 'mp', axis=0, tiled=True)  48.7 us
    all_to_all x1, blocking collectives, local(): lax.all_to_all(input_row_block, 'dp', split_axis=1, concat_axis=0, tiled=...  46.4 us
    reduce_sum x1, other arithmetic, local(): numer = jnp.sum(weighted * both_weights.astype(single_precision), axis=0)  41 us
    reduce_sum x1, other arithmetic, local(): denom = jnp.sum(weighted, axis=0)  35.2 us
  transfers between devices with their start and end apart: 5, of which 1 were waited for; matrix products, arithmetic and copies ran while one was open for 38% of the time, Pallas kernels for 0%

commit v1 on v0

v1 whole, which is shorter than its diff:
```python
import functools
import math

import jax
import jax.numpy as jnp
from jax import lax
from jax.experimental import pallas as pl
from jax.experimental.pallas import tpu as pltpu
from jax.sharding import PartitionSpec as P

LEN = 128
CORES = 2
PIECES = 16
AHEAD = 8
clip_ratio = 0.05
fisher_floor = 0.1
f32 = jnp.float32
bf16 = jnp.bfloat16


def kernel(
    sizes, acts_ref, gate_ref, hid_ref, w_ref, out_ref,
    acts, acts_t, gate, hid, cot, cols_in, w_far, w_own, ratio, merged, part, clips,
    load_sem, own_sem, out_sem,
    w_send, w_recv, c_send, c_recv, a_send, a_recv, z_send, z_recv, k_send, k_recv,
):
    models, seqs, slices = sizes
    m, d, t = lax.axis_index("mp"), lax.axis_index("dp"), lax.axis_index("tensor")
    other = 1 - m
    ys = seqs // CORES
    y, core = d // CORES, d % CORES
    mate = y * CORES + (1 - core)
    width, ff = acts.shape[1], gate.shape[1]
    keep = w_far.shape[0]
    piece = keep // PIECES
    chunk = 2 * piece
    chunks = PIECES // 2
    tile = math.gcd(ff, 512)

    def place(where):
        return dict(zip(("mp", "dp", "tensor"), where))

    def push(src, dst, send, recv, where):
        return pltpu.make_async_remote_copy(
            src_ref=src, dst_ref=dst, send_sem=send, recv_sem=recv,
            device_id=place(where), device_id_type=pl.DeviceIdType.MESH,
        )

    def rest(offset):
        return [(a, b) for a in range(models) for b in range(seqs) if a or b][offset:]

    def plane(a, b):
        return lax.rem(m + a, models), lax.rem(d + b, seqs)

    loads = [
        pltpu.make_async_copy(src, dst, load_sem.at[i])
        for i, (src, dst) in enumerate(((gate_ref, gate), (hid_ref, hid), (acts_ref, acts)))
    ]
    for copy in loads:
        copy.start()

    barrier = pltpu.get_barrier_semaphore()
    for a, b in rest(0):
        pm, pd = plane(a, b)
        pl.semaphore_signal(barrier, inc=1, device_id=place((pm, pd, t)), device_id_type=pl.DeviceIdType.MESH)
    for o in range(1, slices):
        pl.semaphore_signal(
            barrier, inc=1, device_id=place((m, d, lax.rem(t + o, slices))), device_id_type=pl.DeviceIdType.MESH
        )
    pl.semaphore_wait(barrier, models * seqs - 1 + slices - 1)

    def w_piece(k):
        return push(
            w_ref.at[pl.ds(pl.multiple_of(other * keep + k * piece, piece), piece), :],
            w_far.at[pl.ds(pl.multiple_of(k * piece, piece), piece), :],
            w_send.at[k], w_recv.at[k], (other, d, t),
        )

    for k in range(2):
        w_piece(k).start()

    def own_chunk(i):
        slot = lax.rem(i, 2)
        return pltpu.make_async_copy(
            w_ref.at[pl.ds(pl.multiple_of(m * keep + i * chunk, chunk), chunk), :],
            w_own.at[slot], own_sem.at[slot],
        )

    own_chunk(0).start()

    loads[0].wait()
    loads[1].wait()

    @pl.loop(0, ff // tile)
    def _(j):
        at = pl.ds(pl.multiple_of(j * tile, tile), tile)
        v = gate[:, at].astype(f32)
        cot[m, d, :, at] = (hid[:, at].astype(f32) * (v / (1.0 + jnp.exp(-v)))).astype(bf16)

    def cot_to(cm, cs, kind, where):
        return push(cot.at[cm, cs], cot.at[cm, cs], c_send.at[cm, cs, kind], c_recv.at[cm, cs], where)

    def along_y(cm, cs):
        return [cot_to(cm, cs, 1 + o, (m, lax.rem(y + o, ys) * CORES + core, t)) for o in range(1, ys)]

    across = cot_to(m, d, 0, (other, d, t))
    first = [across] + along_y(m, d) + [cot_to(m, d, 1, (m, mate, t))]
    for copy in first:
        copy.start()

    loads[2].wait()
    step = math.gcd(width, 512)

    @pl.loop(0, width // step)
    def _(j):
        at = pl.ds(pl.multiple_of(j * step, step), step)
        acts_t[at, :] = acts[:, at].T

    def block(bm, bd):
        return acts_t.at[pl.ds(pl.multiple_of((bd * models + bm) * keep, keep), keep), :]

    blocks = []
    for a, b in rest(0):
        pm, pd = plane(a, b)
        blocks.append(push(block(pm, pd), cols_in.at[m, d], a_send.at[a, b], a_recv.at[m, d], (pm, pd, t)))
    for copy in blocks:
        copy.start()
    for k in range(2, 4):
        w_piece(k).start()
    cols_in[m, d] = block(m, d)[...]

    def gram(ref, lead, size):
        deep = math.gcd(size, 1024)

        def add(j, total):
            at = pl.ds(pl.multiple_of(j * deep, deep), deep)
            x = ref[:, at] if lead is None else ref[lead[0], lead[1], :, at]
            return total + lax.dot_general(x, x, (((1,), (1,)), ((), ())), preferred_element_type=f32)

        return lax.fori_loop(0, size // deep, add, jnp.zeros((LEN, LEN), f32))

    share = jnp.sum(gram(acts, None, width) * gram(cot, (m, d), ff), axis=(0, 1), keepdims=True)
    part[t] = jnp.broadcast_to(share, part.shape[1:])
    shares = [
        push(part.at[t], part.at[t], z_send.at[o], z_recv.at[t], (m, d, lax.rem(t + o, slices)))
        for o in range(1, slices)
    ]
    for copy in shares:
        copy.start()
    for o in range(1, slices):
        f = lax.rem(t + o, slices)
        push(part.at[f], part.at[f], z_send.at[o], z_recv.at[f], (m, d, f)).wait_recv()
    norm = jnp.sqrt(jnp.sum(part[...], axis=0))
    limit = clip_ratio * math.sqrt(LEN * width * ff * slices)
    factor = limit / jnp.maximum(norm, limit)
    clips[m, d] = factor * factor
    factors = []
    for a, b in rest(0):
        pm, pd = plane(a, b)
        factors.append(push(clips.at[m, d], clips.at[m, d], k_send.at[a, b], k_recv.at[m, d], (pm, pd, t)))
    for copy in factors:
        copy.start()

    def arrived(cm, cs):
        cot_to(cm, cs, 0, (other, d, t)).wait_recv()

    arrived(other, d)
    second = along_y(other, d) + [cot_to(other, d, 1, (m, mate, t))]
    for copy in second:
        copy.start()
    for k in range(4, AHEAD):
        w_piece(k).start()
    third = []
    for cm in (m, other):
        for o in range(1, ys):
            cs = lax.rem(y + o, ys) * CORES + core
            arrived(cm, cs)
            copy = cot_to(cm, cs, 1, (m, mate, t))
            copy.start()
            third.append(copy)
    for cm in (m, other):
        for o in range(ys):
            arrived(cm, lax.rem(y + o, ys) * CORES + (1 - core))
    for a, b in rest(0):
        pm, pd = plane(a, b)
        push(block(pm, pd), cols_in.at[pm, pd], a_send.at[a, b], a_recv.at[pm, pd], (pm, pd, t)).wait_recv()
        push(clips.at[pm, pd], clips.at[pm, pd], k_send.at[a, b], k_recv.at[pm, pd], (pm, pd, t)).wait_recv()

    def out_chunk(i):
        slot = lax.rem(i, 2)
        return pltpu.make_async_copy(
            merged.at[slot], out_ref.at[pl.ds(pl.multiple_of(i * chunk, chunk), chunk), :], out_sem.at[slot]
        )

    @pl.loop(0, chunks)
    def _(i):
        slot = lax.rem(i, 2)
        rows = pl.ds(pl.multiple_of(i * chunk, chunk), chunk)

        @pl.when(i >= 1)
        def _():
            w_piece(2 * i - 2).wait_send()
            w_piece(2 * i - 1).wait_send()

        @pl.when((2 * i + 2 >= AHEAD) & (2 * i + 2 < PIECES))
        def _():
            w_piece(2 * i + 2).start()
            w_piece(2 * i + 3).start()

        @pl.when(i + 1 < chunks)
        def _():
            own_chunk(i + 1).start()

        @pl.loop(0, ff // tile)
        def _(j):
            at = pl.ds(pl.multiple_of(j * tile, tile), tile)

            def weight(fm):
                total = jnp.full((chunk, tile), fisher_floor, f32)
                fisher = None
                for s in range(seqs):
                    grad = jnp.dot(cols_in[fm, s, rows, :], cot[fm, s, :, at], preferred_element_type=f32)
                    term = clips[fm, s, 0:1, 0:1] * (grad * grad)
                    fisher = term if fisher is None else fisher + term
                return fisher + total

            far = weight(other)
            ratio[:, at] = far / (far + weight(m))

        own_chunk(i).wait()

        @pl.when(i >= 2)
        def _():
            out_chunk(i - 2).wait()

        w_piece(2 * i).wait_recv()
        w_piece(2 * i + 1).wait_recv()

        @pl.loop(0, ff // tile)
        def _(j):
            at = pl.ds(pl.multiple_of(j * tile, tile), tile)
            near = w_own[slot, :, at].astype(f32)
            far = w_far[rows, at].astype(f32)
            merged[slot, :, at] = (near + ratio[:, at] * (far - near)).astype(bf16)

        out_chunk(i).start()

    for k in range(PIECES - 2, PIECES):
        w_piece(k).wait_send()
    for copy in first + second + third + blocks + shares + factors:
        copy.wait_send()
    for i in range(chunks - 2, chunks):
        out_chunk(i).wait()


def solution(mesh):
    models, seqs, slices = mesh.shape["mp"], mesh.shape["dp"], mesh.shape["tensor"]

    def local(activations, gate_pre, hidden_grad, up_weights):
        tokens, width = activations.shape[1:]
        ff = gate_pre.shape[2]
        keep = up_weights.shape[1] // models
        chunk = keep // PIECES * 2
        assert tokens == LEN and models == 2 and seqs % CORES == 0
        dma, vmem = pltpu.SemaphoreType.DMA, pltpu.VMEM
        return pl.pallas_call(
            functools.partial(kernel, (models, seqs, slices)),
            out_shape=jax.ShapeDtypeStruct((keep, ff), bf16),
            in_specs=[pl.BlockSpec(memory_space=pl.ANY)] * 4,
            out_specs=pl.BlockSpec(memory_space=pl.ANY),
            scratch_shapes=[
                vmem((LEN, width), bf16),
                vmem((width, LEN), bf16),
                vmem((LEN, ff), bf16),
                vmem((LEN, ff), bf16),
                vmem((models, seqs, LEN, ff), bf16),
                vmem((models, seqs, keep, LEN), bf16),
                vmem((keep, ff), bf16),
                vmem((2, chunk, ff), bf16),
                vmem((chunk, ff), f32),
                vmem((2, chunk, ff), bf16),
                vmem((slices, 8, 128), f32),
                vmem((models, seqs, 8, 128), f32),
                dma((3,)),
                dma((2,)),
                dma((2,)),
                dma((PIECES,)),
                dma((PIECES,)),
                dma((models, seqs, 1 + seqs // CORES)),
                dma((models, seqs)),
                dma((models, seqs)),
                dma((models, seqs)),
                dma((slices,)),
                dma((slices,)),
                dma((models, seqs)),
                dma((models, seqs)),
            ],
            compiler_params=pltpu.CompilerParams(
                collective_id=0, has_side_effects=True, vmem_limit_bytes=58 * 2**20
            ),
        )(activations[0], gate_pre[0], hidden_grad[0], up_weights[0])

    placed = (
        P("mp", "dp", None),
        P("mp", "dp", "tensor"),
        P("mp", "dp", "tensor"),
        P("mp", "dp", "tensor"),
    )
    return jax.shard_map(
        local, mesh=mesh, in_specs=placed, out_specs=P(("dp", "mp"), "tensor"), check_vma=False
    )
```

time: 1120 us -> 400 us (0.36)
  Pallas kernels: 0 us -> 387 us
  blocking collectives: 362 us -> 0 us
  other arithmetic: 293 us -> 0 us
  local copies, waits for them, and re-layouts: 224 us -> 13.2 us
  matrix products: 150 us -> 0 us
  waiting for transfers between devices: 48.7 us -> 0 us
  starting transfers between devices: 16.6 us -> 0 us
  between operations: 15.9 us -> 0.01 us
    pallas_call x0 -> x1, Pallas kernels: none -> 387 us  [local(): pl.pallas_call(functools.partial(kernel, (models, seqs, slices)), out_sha...]
    unnamed x1 -> x0, blocking collectives: 311 us -> none
    unnamed x3 -> x0, other arithmetic: 187 us -> none
    unnamed x15 -> x1, local copies, waits for them, and re-layouts: 179 us -> 13.2 us
    dot_general x6 -> x0, matrix products: 150 us -> none  [the longest x4 141 us: one_seq(): jnp.einsum('mld,mlf->mdf', acts_models[:, seq_index], cot_piece[:, seq_in...]
    reduce_sum x2 -> x0, other arithmetic: 76.2 us -> none  [the longest x1 41 us: local(): numer = jnp.sum(weighted * both_weights.astype(single_precision), axis=0)]
    all_gather x2 -> x0, waiting for transfers between devices: 48.7 us -> none  [the longest x1 48.7 us: local(): lax.all_gather(cot_seq[None], 'mp', axis=0, tiled=True)]
    all_to_all x1 -> x0, blocking collectives: 46.4 us -> none  [local(): lax.all_to_all(input_row_block, 'dp', split_axis=1, concat_axis=0, tiled=...]
  transfers between devices with their start and end apart: 5 -> 0, of which waited for: 1 -> 0; matrix products, arithmetic and copies ran while one was open for 38% -> 0% of each run, Pallas kernels for 0% -> 0%
where the time goes in v1:
time: 400 us
  Pallas kernels  387 us (97%)
  local copies, waits for them, and re-layouts  13.2 us (3%)
    pallas_call x1, Pallas kernels, local(): pl.pallas_call(functools.partial(kernel, (models, seqs, slices)), out_sha...  387 us
    unnamed x1, local copies, waits for them, and re-layouts  13.2 us

profile of v1, /device:TPU:0, one launch (start us, length us, event | category | flops | bytes accessed | tf_op | source)
XLA Modules:
  0.0 400.2 jit_solution(4728579231243184734)
XLA Ops:
  0.0 387.0 %shard_map.46 = bf16[1024,7168]{1,0:T(8,128)(2,1)} custom-call(bf16[128,8192]{1,0:T(8,128)(2,1)} %bitcast.5, bf16[128,7168]{1,0:T(8,128)(2,1)} %bitcast.6, bf16[128,7168]{1,0:T(8,128)(2,1)} %bitcast.7, bf16[2048,7168]{1,0:T(8,128)(2,1)} %bitcast.4), custom_call_target="tpu_custom_call" | custom-call | tf_op jit(solution)/shard_map/pallas_call | solution.py:266
  387.0 13.2 %copy.6 = bf16[1024,7168]{1,0:T(8,128)(2,1)} copy(bf16[1024,7168]{1,0:T(8,128)(2,1)} %shard_map.46) | data formatting | bytes 29360128

commit v2 on v1

--- a/solution.py
+++ b/solution.py
@@ -22,7 +22,7 @@
     sizes, acts_ref, gate_ref, hid_ref, w_ref, out_ref,
     acts, acts_t, gate, hid, cot, cols_in, w_far, w_own, ratio, merged, part, clips,
     load_sem, own_sem, out_sem,
-    w_send, w_recv, c_send, c_recv, a_send, a_recv, z_send, z_recv, k_send, k_recv,
+    w_send, w_recv, c_send, c_recv, a_send, a_recv, g_send, g_recv, z_send, z_recv, k_send, k_recv,
 ):
     models, seqs, slices = sizes
     m, d, t = lax.axis_index("mp"), lax.axis_index("dp"), lax.axis_index("tensor")
@@ -116,13 +116,26 @@
         at = pl.ds(pl.multiple_of(j * step, step), step)
         acts_t[at, :] = acts[:, at].T
 
+    sub = keep // slices
+
     def block(bm, bd):
         return acts_t.at[pl.ds(pl.multiple_of((bd * models + bm) * keep, keep), keep), :]
 
-    blocks = []
-    for a, b in rest(0):
+    def rows_of(a, b, sm, sd):
         pm, pd = plane(a, b)
-        blocks.append(push(block(pm, pd), cols_in.at[m, d], a_send.at[a, b], a_recv.at[m, d], (pm, pd, t)))
+        if a == 0:
+            return push(block(pm, pd), cols_in.at[sm, sd], a_send.at[a, b], a_recv.at[sm, sd], (pm, pd, t))
+        mine = pl.ds(pl.multiple_of(t * sub, sub), sub)
+        return push(
+            block(pm, pd).at[mine, :], cols_in.at[sm, sd, mine, :], a_send.at[a, b], a_recv.at[sm, sd], (pm, pd, t)
+        )
+
+    def shared(part_of, o):
+        at = pl.ds(pl.multiple_of(part_of * sub, sub), sub)
+        ref = cols_in.at[other, :, at, :]
+        return push(ref, ref, g_send.at[o], g_recv.at[part_of], (m, d, lax.rem(t + o, slices)))
+
+    blocks = [rows_of(a, b, m, d) for a, b in rest(0)]
     for copy in blocks:
         copy.start()
     for k in range(2, 4):
@@ -170,6 +183,12 @@
         copy.start()
     for k in range(4, AHEAD):
         w_piece(k).start()
+    for a, b in rest(0):
+        if a:
+            rows_of(a, b, *plane(a, b)).wait_recv()
+    passed = [shared(t, o) for o in range(1, slices)]
+    for copy in passed:
+        copy.start()
     third = []
     for cm in (m, other):
         for o in range(1, ys):
@@ -183,8 +202,12 @@
             arrived(cm, lax.rem(y + o, ys) * CORES + (1 - core))
     for a, b in rest(0):
         pm, pd = plane(a, b)
-        push(block(pm, pd), cols_in.at[pm, pd], a_send.at[a, b], a_recv.at[pm, pd], (pm, pd, t)).wait_recv()
+        if a == 0:
+            rows_of(a, b, pm, pd).wait_recv()
         push(clips.at[pm, pd], clips.at[pm, pd], k_send.at[a, b], k_recv.at[pm, pd], (pm, pd, t)).wait_recv()
+
+    for o in range(1, slices):
+        shared(lax.rem(t + o, slices), o).wait_recv()
 
     def out_chunk(i):
         slot = lax.rem(i, 2)
@@ -233,21 +256,23 @@
         def _():
             out_chunk(i - 2).wait()
 
-        w_piece(2 * i).wait_recv()
-        w_piece(2 * i + 1).wait_recv()
-
-        @pl.loop(0, ff // tile)
-        def _(j):
-            at = pl.ds(pl.multiple_of(j * tile, tile), tile)
-            near = w_own[slot, :, at].astype(f32)
-            far = w_far[rows, at].astype(f32)
-            merged[slot, :, at] = (near + ratio[:, at] * (far - near)).astype(bf16)
+        for half in range(2):
+            w_piece(2 * i + half).wait_recv()
+            part_rows = pl.ds(half * piece, piece)
+            far_rows = pl.ds(pl.multiple_of(i * chunk + half * piece, piece), piece)
+
+            @pl.loop(0, ff // tile)
+            def _(j):
+                at = pl.ds(pl.multiple_of(j * tile, tile), tile)
+                near = w_own[slot, part_rows, at].astype(f32)
+                far = w_far[far_rows, at].astype(f32)
+                merged[slot, part_rows, at] = (near + ratio[part_rows, at] * (far - near)).astype(bf16)
 
         out_chunk(i).start()
 
     for k in range(PIECES - 2, PIECES):
         w_piece(k).wait_send()
-    for copy in first + second + third + blocks + shares + factors:
+    for copy in first + second + third + blocks + passed + shares + factors:
         copy.wait_send()
     for i in range(chunks - 2, chunks):
         out_chunk(i).wait()
@@ -292,6 +317,8 @@
                 dma((models, seqs)),
                 dma((slices,)),
                 dma((slices,)),
+                dma((slices,)),
+                dma((slices,)),
                 dma((models, seqs)),
                 dma((models, seqs)),
             ],

time: 400 us -> 383 us (0.958)
  Pallas kernels: 387 us -> 370 us
    pallas_call x1, Pallas kernels: 387 us -> 370 us  [local(): pl.pallas_call(functools.partial(kernel, (models, seqs, slices)), out_sha...]
where the time goes in v2:
time: 383 us
  Pallas kernels  370 us (97%)
  local copies, waits for them, and re-layouts  13.2 us (3%)
    pallas_call x1, Pallas kernels, local(): pl.pallas_call(functools.partial(kernel, (models, seqs, slices)), out_sha...  370 us
    unnamed x1, local copies, waits for them, and re-layouts  13.2 us

profile of v2, /device:TPU:0, one launch (start us, length us, event | category | flops | bytes accessed | tf_op | source)
XLA Modules:
  0.0 383.0 jit_solution(15216545948056663665)
XLA Ops:
  0.0 369.8 %shard_map.46 = bf16[1024,7168]{1,0:T(8,128)(2,1)} custom-call(bf16[128,8192]{1,0:T(8,128)(2,1)} %bitcast.5, bf16[128,7168]{1,0:T(8,128)(2,1)} %bitcast.6, bf16[128,7168]{1,0:T(8,128)(2,1)} %bitcast.7, bf16[2048,7168]{1,0:T(8,128)(2,1)} %bitcast.4), custom_call_target="tpu_custom_call" | custom-call | tf_op jit(solution)/shard_map/pallas_call | solution.py:291
  369.8 13.2 %copy.6 = bf16[1024,7168]{1,0:T(8,128)(2,1)} copy(bf16[1024,7168]{1,0:T(8,128)(2,1)} %shard_map.46) | data formatting | bytes 29360128
